TPU v7x, 512 devices: a whole 4x4x16 slice. The times are simulated.
512 devices in a mesh: tm: 32 (over z, core), dp: 8 (over x_lo, y), rep: 2 (over x_hi).
Axes of the slice: x: 4 (x_hi: 2, x_lo: 2; x = x_hi * 2 + x_lo), y: 4, z: 16, core: 2. Of those that a mesh axis runs over, the one named last changes fastest.
Arguments:
- clip_frames: bfloat16 [16, 128, 32, 4, 256], P(('dp', 'rep'), 'tm'), may hold values from -6 to 6
- conv_weight: bfloat16 [3, 3, 3, 256, 256], replicated, may hold values from -0.078125 to 0.078125
- up_weight: bfloat16 [256, 1024], replicated, may hold values from -0.375 to 0.375
- cotangent: bfloat16 [16, 128, 32, 4, 1024], P(('dp', 'rep'), None, 'tm'), may hold values from -6 to 6
Outputs:
- input_grad: bfloat16 [16, 128, 32, 4, 256], P(('dp', 'rep'), 'tm')
- up_grad: float32 [256, 1024], P('tm', ('dp', 'rep'))
All inputs are finite; a program needn't handle non-finite values.
Results may differ from a plain program's by a relative error of at most 0.012.
Values may be sent and summed in bfloat16 or wider, within the bound.
A program may use at most 128 MiB of HBM per device.

v0:
```python
import math
import jax
import jax.numpy as jnp
from jax import lax
from jax.sharding import PartitionSpec as P


def from_behind(value, axis, steps):
    count = lax.axis_size(axis)
    initial, last = (max(0, -steps), min(count, count - steps))
    return lax.ppermute(value, axis, [(source, source + steps) for source in range(initial, last)])


def correlate(source, kernel, frames):
    rows = source.shape[1] - 2
    cols = source.shape[2] - 2
    patches = []
    for shift_t in range(3):
        for shift_r in range(3):
            for shift_c in range(3):
                patches.append(
                    source[
                        shift_t : shift_t + frames,
                        shift_r : shift_r + rows,
                        shift_c : shift_c + cols,
                    ]
                )
    stacked = jnp.concatenate(patches, axis=-1)
    width = stacked.shape[-1]
    flat_kernel = kernel.reshape(width, kernel.shape[-1])
    return jnp.dot(stacked.reshape(-1, width), flat_kernel, preferred_element_type=jnp.float32)


def pad_space(field):
    return jnp.pad(field, ((0, 0), (1, 1), (1, 1), (0, 0)))


def local(clip_frames, conv_weight, up_weight, cotangent):
    frames_local = clip_frames[0]
    frames = frames_local.shape[0]
    rows = frames_local.shape[1]
    cols = frames_local.shape[2]
    chans = frames_local.shape[3]
    is_first = lax.axis_index("tm") == 0
    earlier = from_behind(frames_local[frames - 2 :], "tm", 1)
    earlier = jnp.where(is_first, jnp.broadcast_to(frames_local[:1], earlier.shape), earlier)
    source = pad_space(jnp.concatenate([earlier, frames_local], axis=0))
    pre = correlate(source, conv_weight, frames)
    hidden = jax.nn.silu(pre).astype(jnp.bfloat16).reshape(1, frames, rows, cols, chans)
    contract_rows = (((0,), (0,)), ((), ()))
    contract_cols = (((1,), (1,)), ((), ()))
    row_hidden = lax.all_to_all(hidden, "tm", split_axis=2, concat_axis=1, tiled=True)
    flat_h = row_hidden.reshape(-1, chans)
    flat_g = cotangent.reshape(-1, cotangent.shape[-1])
    term = lax.dot_general(flat_h, flat_g, contract_rows, preferred_element_type=jnp.float32)
    row_grad = lax.dot_general(
        flat_g, up_weight, contract_cols, preferred_element_type=jnp.float32
    ).astype(jnp.bfloat16)
    hidden_grad = lax.all_to_all(
        row_grad.reshape(row_hidden.shape), "tm", split_axis=1, concat_axis=2, tiled=True
    )
    sigma = jax.nn.sigmoid(pre)
    slope = sigma * (1.0 + pre * (1.0 - sigma))
    pre_grad = (hidden_grad.reshape(-1, chans).astype(jnp.float32) * slope).astype(jnp.bfloat16)
    pre_grad = pre_grad.reshape(frames, rows, cols, chans)
    later = from_behind(pre_grad[:2], "tm", -1)
    back_kernel = jnp.transpose(conv_weight[::-1, ::-1, ::-1], (0, 1, 2, 4, 3))
    grad_source = pad_space(jnp.concatenate([pre_grad, later], axis=0))
    input_grad = correlate(grad_source, back_kernel, frames).reshape(frames, rows, cols, chans)

    def edge_term():
        start = jnp.concatenate(
            [jnp.zeros((2, rows, cols, chans), jnp.bfloat16), pre_grad[:2]], axis=0
        )
        parts = correlate(pad_space(start), back_kernel, 2).reshape(2, rows, cols, chans)
        return parts[0] + parts[1]

    def no_term():
        return jnp.zeros((rows, cols, chans), jnp.float32)

    edge = lax.cond(is_first, edge_term, no_term)
    input_grad = input_grad.at[0].add(edge)
    time_count = lax.axis_size("tm")
    clip_count = lax.axis_size(("dp", "rep"))
    factor = 1.0 / math.sqrt(clip_count * frames * time_count * rows * cols)
    part = lax.psum_scatter(term, "tm", scatter_dimension=0, tiled=True)
    summed = lax.psum_scatter(part, ("dp", "rep"), scatter_dimension=1, tiled=True)
    return (input_grad.astype(jnp.bfloat16)[None], summed * factor)


def solution(mesh):
    in_specs = (
        P(("dp", "rep"), "tm", None, None, None),
        P(),
        P(),
        P(("dp", "rep"), None, "tm", None, None),
    )
    out_specs = (P(("dp", "rep"), "tm", None, None, None), P("tm", ("dp", "rep")))
    return jax.shard_map(local, mesh=mesh, in_specs=in_specs, out_specs=out_specs, check_vma=False)
```

profile of v0, /device:TPU:32, one launch (start us, length us, event | category | flops | bytes accessed | tf_op | source)
XLA Modules:
  0.0 382.3 jit_solution(11873751514262837852)
XLA Ops:
  8.2 1.9 collective-permute-start
  12.7 16.1 %all-to-all-start = ((bf16[1,128,1,4,256]{4,3,2,0,1:T(4,128)(2,1)}), bf16[1,128,1,4,256]{4,3,2,0,1:T(4,128)(2,1)S(1)}, u32[]{:S(2)}, u32[]{:S(2)}) async-start(bf16[1,128,1,4,256]{4,3,2,0,1:T(4,128)(2,1)} %bitcast.1), calls=%async_computation | async-start | bytes 524288 | tf_op jit(solution)/shard_map/all_to_all | solution.py:59
  30.7 6.0 %copy.26 = bf16[3,3,3,256,256]{3,4,2,1,0:T(8,128)(2,1)} copy(bf16[3,3,3,256,256]{4,3,2,1,0:T(8,128)(2,1)} %param.9) | data formatting | bytes 7077888 | tf_op args[1]
  36.7 4.3 %rev.3 = bf16[3,3,3,256,256]{3,4,2,1,0:T(8,128)(2,1)} reverse(bf16[3,3,3,256,256]{3,4,2,1,0:T(8,128)(2,1)} %copy.26), dimensions={0,1,2} | reverse | bytes 7077888 | tf_op jit(solution)/shard_map/rev | solution.py:67
  41.0 4.2 %reverse_bitcast_fusion = bf16[3,3,3,256,256]{4,3,2,1,0:T(8,128)(2,1)} fusion(bf16[3,3,3,256,256]{3,4,2,1,0:T(8,128)(2,1)} %copy.26), kind=kLoop, calls=%fused_computation.175 | loop fusion | bytes 7077888 | tf_op jit(solution)/shard_map/transpose | solution.py:67
  45.5 4.1 %pad_slice_fusion.24 = (bf16[4,32,4,256]{3,2,1,0:T(4,128)(2,1)}, bf16[4,32,4,256]{3,2,1,0:T(4,128)(2,1)}, bf16[4,32,4,256]{3,2,1,0:T(4,128)(2,1)}, bf16[4,32,4,2...) fusion(bf16[6,32,4,256]{3,2,1,0:T(4,128)(2,1)S(1)} %pad_maximum, ...), kind=kLoop, calls=%fused_computation.52 | loop fusion | bytes 5373952 | tf_op jit(solution)/shard_map/slice | solution.py:22
  51.5 1.7 concatenate.77
  54.0 1.8 concatenate.78
  55.8 1.7 concatenate.79
  58.3 1.7 concatenate.81
  66.9 1.7 concatenate.86
  70.3 1.7 concatenate.88
  72.8 1.7 concatenate.90
  76.2 1.7 concatenate.92
  86.1 1.8 constant_dynamic-update-slice_fusion.26
  87.9 1.7 constant_dynamic-update-slice_fusion.25
  119.5 6.1 %multiply_convert_fusion = (bf16[512,256]{1,0:T(8,128)(2,1)S(1)}, bf16[512,256]{1,0:T(8,128)(2,1)S(1)}) fusion(f32[512,256]{1,0:T(8,128)S(1)} %reshape.138, bf16[512,6912]{1,0:T(8,128)(2,1)} %constant_dynamic-update-slice_fusion.1, bf16[6912,256]{1,0:T(8,128)(2,1)} %bitcast.46), kind=kOutput, calls=%fused_computation.102 | convolution fusion | flops 1813381120 | bytes 11665408 | tf_op jit(solution)/shard_map/dot_general | solution.py:31
  125.7 2.0 collective-permute-start.1
  128.6 12.4 %all-to-all-start.1 = ((bf16[1,4,32,4,256]{4,3,1,0,2:T(4,128)(2,1)}), bf16[1,4,32,4,256]{4,3,1,0,2:T(4,128)(2,1)S(1)}, u32[]{:S(2)}, u32[]{:S(2)}) async-start(bf16[1,4,32,4,256]{4,3,1,0,2:T(4,128)(2,1)} %copy.28), calls=%async_computation.1 | async-start | bytes 524288 | tf_op jit(solution)/shard_map/all_to_all | solution.py:52
  156.2 5.8 %all-to-all-done.1 = bf16[1,4,32,4,256]{4,3,1,0,2:T(4,128)(2,1)S(1)} async-done(((bf16[1,4,32,4,256]{4,3,1,0,2:T(4,128)(2,1)}), bf16[1,4,32,4,256]{4,3,1,0,2:T(4,128)(2,1)S(1)}, u32[]{:S(2)}, u32[]{:S(2)}) %all-to-all-start.1) | async-done | bytes 262176 | tf_op jit(solution)/shard_map/all_to_all | solution.py:52
  170.0 6.0 %fusion.52 = f32[4,32,4,256]{3,1,2,0:T(8,128)S(1)} fusion(bf16[4,32,4,6912]{3,1,2,0:T(8,128)(2,1)} %fusion.49, bf16[6912,256,1,1]{1,0,3,2:T(8,128)(2,1)} %bitcast.47), kind=kOutput, calls=%fused_computation.177 | convolution fusion | flops 1811939328 | bytes 11141120 | tf_op jit(solution)/shard_map/dot_general | solution.py:31
  176.0 109.4 %reduce-scatter.5.cloned.1.call-done = f32[8,1024]{1,0:T(8,128)} async-done(((f32[256,1024]{1,0:T(8,128)}), f32[8,1024]{1,0:T(8,128)}) %reduce-scatter.5.cloned.1.call-update) | async-done | bytes 32784 | tf_op jit(solution)/shard_map/reduce_scatter | solution.py:86
  285.4 1.8 copy.31
  288.1 86.0 %reduce-scatter.7.cloned.1.call-done = f32[64,8]{1,0:T(8,128)} async-done(((f32[1024,8]{1,0:T(8,128)}), f32[64,8]{1,0:T(8,128)}) %reduce-scatter.7.cloned.1.call-update) | async-done | bytes 2064
  (128 shorter events, 84.6 us)
Async XLA Ops:
  7.2 4.3 %copy-start = (bf16[256,1024]{1,0:T(8,128)(2,1)S(1)}, bf16[256,1024]{1,0:T(8,128)(2,1)}, u32[]{:S(2)}) copy-start(bf16[256,1024]{1,0:T(8,128)(2,1)} %param.10) | copy-start | bytes 1572868
  8.2 37.1 %collective-permute-start = (bf16[2,32,4,256]{3,2,1,0:T(4,128)(2,1)S(1)}, bf16[2,32,4,256]{3,2,1,0:T(4,128)(2,1)S(1)}, u32[]{:S(2)}, u32[]{:S(2)}) collective-permute-start(bf16[2,32,4,256]{3,2,1,0:T(4,128)(2,1)S(1)} %slice_bitcast_fusion), channel_id=1, source_target_pairs={{0,16},{16,32},{32,48},{48,64},{64,80},{80,96},{96,112},{112,128},... | collective-permute-start | bytes 393224 | tf_op jit(solution)/shard_map/ppermute | solution.py:11
  12.7 106.5 %all-to-all-start = ((bf16[1,128,1,4,256]{4,3,2,0,1:T(4,128)(2,1)}), bf16[1,128,1,4,256]{4,3,2,0,1:T(4,128)(2,1)S(1)}, u32[]{:S(2)}, u32[]{:S(2)}) async-start(bf16[1,128,1,4,256]{4,3,2,0,1:T(4,128)(2,1)} %bitcast.1), calls=%async_computation | async-start | bytes 524288 | tf_op jit(solution)/shard_map/all_to_all | solution.py:59
  36.7 8.6 %copy-start.1 = (bf16[1,4,32,4,256]{4,3,2,1,0:T(4,128)(2,1)S(1)}, bf16[1,4,32,4,256]{4,3,2,1,0:T(4,128)(2,1)}, u32[]{:S(2)}) copy-start(bf16[1,4,32,4,256]{4,3,2,1,0:T(4,128)(2,1)} %param.8) | copy-start | bytes 786436
  53.3 29.8 %copy-start.10 = (bf16[4,32,4,256]{3,2,1,0:T(4,128)(2,1)S(1)}, bf16[4,32,4,256]{3,2,1,0:T(4,128)(2,1)}, u32[]{:S(2)}) copy-start(bf16[4,32,4,256]{3,2,1,0:T(4,128)(2,1)} %get-tuple-element.51) | copy-start | bytes 786436
  54.0 29.9 %copy-start.8 = (bf16[4,32,4,256]{3,2,1,0:T(4,128)(2,1)S(1)}, bf16[4,32,4,256]{3,2,1,0:T(4,128)(2,1)}, u32[]{:S(2)}) copy-start(bf16[4,32,4,256]{3,2,1,0:T(4,128)(2,1)} %get-tuple-element.55) | copy-start | bytes 786436
  58.3 25.6 %copy-start.9 = (bf16[4,32,4,256]{3,2,1,0:T(4,128)(2,1)S(1)}, bf16[4,32,4,256]{3,2,1,0:T(4,128)(2,1)}, u32[]{:S(2)}) copy-start(bf16[4,32,4,256]{3,2,1,0:T(4,128)(2,1)} %get-tuple-element.54) | copy-start | bytes 786436
  86.1 23.9 %copy-start.7 = (bf16[512,256]{1,0:T(8,128)(2,1)S(1)}, bf16[512,256]{1,0:T(8,128)(2,1)}, u32[]{:S(2)}) copy-start(bf16[512,256]{1,0:T(8,128)(2,1)} %concatenate.91) | copy-start | bytes 786436
  86.1 24.7 %copy-start.6 = (bf16[512,256]{1,0:T(8,128)(2,1)S(1)}, bf16[512,256]{1,0:T(8,128)(2,1)}, u32[]{:S(2)}) copy-start(bf16[512,256]{1,0:T(8,128)(2,1)} %concatenate.92) | copy-start | bytes 786436
  86.1 25.4 %copy-start.5 = (bf16[512,256]{1,0:T(8,128)(2,1)S(1)}, bf16[512,256]{1,0:T(8,128)(2,1)}, u32[]{:S(2)}) copy-start(bf16[512,256]{1,0:T(8,128)(2,1)} %concatenate.93) | copy-start | bytes 786436
  86.1 26.2 %copy-start.4 = (bf16[512,256]{1,0:T(8,128)(2,1)S(1)}, bf16[512,256]{1,0:T(8,128)(2,1)}, u32[]{:S(2)}) copy-start(bf16[512,256]{1,0:T(8,128)(2,1)} %concatenate.94) | copy-start | bytes 786436
  86.1 26.9 %copy-start.3 = (bf16[512,256]{1,0:T(8,128)(2,1)S(1)}, bf16[512,256]{1,0:T(8,128)(2,1)}, u32[]{:S(2)}) copy-start(bf16[512,256]{1,0:T(8,128)(2,1)} %concatenate.95) | copy-start | bytes 786436
  86.1 27.7 %copy-start.2 = (bf16[512,256]{1,0:T(8,128)(2,1)S(1)}, bf16[512,256]{1,0:T(8,128)(2,1)}, u32[]{:S(2)}) copy-start(bf16[512,256]{1,0:T(8,128)(2,1)} %concatenate.96) | copy-start | bytes 786436
  125.7 15.6 %collective-permute-start.1 = (bf16[2,32,4,256]{3,1,2,0:T(8,128)(2,1)S(1)}, bf16[2,32,4,256]{3,1,2,0:T(8,128)(2,1)S(1)}, u32[]{:S(2)}, u32[]{:S(2)}) collective-permute-start(bf16[2,32,4,256]{3,1,2,0:T(8,128)(2,1)S(1)} %copy.23), channel_id=1, source_target_pairs={{16,0},{32,16},{48,32},{64,48},{80,64},{96,80},{112,96},{128,112},... | collective-permute-start | bytes 393224 | tf_op jit(solution)/shard_map/ppermute | solution.py:11
  128.6 33.4 %all-to-all-start.1 = ((bf16[1,4,32,4,256]{4,3,1,0,2:T(4,128)(2,1)}), bf16[1,4,32,4,256]{4,3,1,0,2:T(4,128)(2,1)S(1)}, u32[]{:S(2)}, u32[]{:S(2)}) async-start(bf16[1,4,32,4,256]{4,3,1,0,2:T(4,128)(2,1)} %copy.28), calls=%async_computation.1 | async-start | bytes 524288 | tf_op jit(solution)/shard_map/all_to_all | solution.py:52
  141.0 144.3 %reduce-scatter.5.cloned.1.call-start = ((), (), s32[]{:S(2)}) async-start(), calls=%async_computation.4 | async-start | bytes 1081344 | tf_op jit(solution)/shard_map/reduce_scatter | solution.py:86
  163.5 210.5 %reduce-scatter.7.cloned.1.call-start = ((), (), s32[]{:S(2)}) async-start(), calls=%async_computation.5 | async-start | bytes 557056
Sparse Core Ops, SparseCore 0:
  163.7 121.6 reduce-scatter.4
  288.4 85.6 reduce-scatter.6
where the time goes:
time: 384 us; the launch traced here: 382 us
  waiting for transfers between devices  201 us (52%)
  local copies, waits for them, and re-layouts  119 us (31%)
  starting transfers between devices  32.5 us (8%)
  between operations  14.4 us (4%)
  matrix products  14 us (4%)
    reduce_scatter x1, waiting for transfers between devices, local(): part = lax.psum_scatter(term, 'tm', scatter_dimension=0, tiled=True)  109 us
    unnamed x3, waiting for transfers between devices  86 us
    unnamed x79, local copies, waits for them, and re-layouts  63 us
    concatenate x29, local copies, waits for them, and re-layouts, correlate(): stacked = jnp.concatenate(patches, axis=-1)  36.3 us
    all_to_all x1, starting transfers between devices, local(): lax.all_to_all(row_grad.reshape(row_hidden.shape), 'tm', split_axis=1, co...  16.1 us
    all_to_all x1, starting transfers between devices, local(): lax.all_to_all(hidden, 'tm', split_axis=2, concat_axis=1, tiled=True)  12.4 us
    dot_general x2, matrix products, correlate(): jnp.dot(stacked.reshape(-1, width), flat_kernel, preferred_element_type=j...  12.1 us
  transfers between devices with their start and end apart: 6, of which 3 were waited for; matrix products, arithmetic and copies ran while one was open for 32% of the time, Pallas kernels for 0%

commit v1 on v0

--- a/solution.py
+++ b/solution.py
@@ -49,7 +49,10 @@
     hidden = jax.nn.silu(pre).astype(jnp.bfloat16).reshape(1, frames, rows, cols, chans)
     contract_rows = (((0,), (0,)), ((), ()))
     contract_cols = (((1,), (1,)), ((), ()))
-    row_hidden = lax.all_to_all(hidden, "tm", split_axis=2, concat_axis=1, tiled=True)
+    row_hidden = jnp.concatenate(
+        lax.all_to_all(jnp.stack(jnp.split(hidden, lax.axis_size("tm"), axis=2)), "tm", 0, 0),
+        axis=1,
+    )
     flat_h = row_hidden.reshape(-1, chans)
     flat_g = cotangent.reshape(-1, cotangent.shape[-1])
     term = lax.dot_general(flat_h, flat_g, contract_rows, preferred_element_type=jnp.float32)

time: 384 us -> 402 us (1.047)
  local copies, waits for them, and re-layouts: 119 us -> 137 us
    unnamed x79 -> x110, local copies, waits for them, and re-layouts: 63 us -> 81.7 us
    ppermute x2, waiting for transfers between devices: 0.01 us -> 9.96 us  [from_behind(): lax.ppermute(value, axis, [(source, source + steps) for source in range(i...]
    all_to_all x1, waiting for transfers between devices: 5.79 us -> 0.01 us  [local(): lax.all_to_all(jnp.stack(jnp.split(hidden, lax.axis_size('tm'), axis=2)),...]
    reduce_scatter x1, waiting for transfers between devices: 109 us -> 104 us  [local(): part = lax.psum_scatter(term, 'tm', scatter_dimension=0, tiled=True)]
  transfers between devices with their start and end apart: 6 -> 6, of which waited for: 3 -> 3; matrix products, arithmetic and copies ran while one was open for 32% -> 30% of each run, Pallas kernels for 0% -> 0%
where the time goes in v1:
time: 402 us; the launch traced here: 400 us
  waiting for transfers between devices  200 us (50%)
  local copies, waits for them, and re-layouts  137 us (34%)
  starting transfers between devices  32.3 us (8%)
  between operations  14.4 us (4%)
  matrix products  14 us (3%)
    reduce_scatter x1, waiting for transfers between devices, local(): part = lax.psum_scatter(term, 'tm', scatter_dimension=0, tiled=True)  104 us
    unnamed x3, waiting for transfers between devices  86 us
    unnamed x110, local copies, waits for them, and re-layouts  81.7 us
    concatenate x29, local copies, waits for them, and re-layouts, correlate(): stacked = jnp.concatenate(patches, axis=-1)  36.3 us
    all_to_all x1, starting transfers between devices, local(): lax.all_to_all(row_grad.reshape(row_hidden.shape), 'tm', split_axis=1, co...  16.1 us
    all_to_all x1, starting transfers between devices, local(): lax.all_to_all(jnp.stack(jnp.split(hidden, lax.axis_size('tm'), axis=2)),...  12.2 us
    dot_general x2, matrix products, correlate(): jnp.dot(stacked.reshape(-1, width), flat_kernel, preferred_element_type=j...  12.1 us
    ppermute x2, waiting for transfers between devices, from_behind(): lax.ppermute(value, axis, [(source, source + steps) for source in range(i...  9.96 us
  transfers between devices with their start and end apart: 6, of which 3 were waited for; matrix products, arithmetic and copies ran while one was open for 30% of the time, Pallas kernels for 0%

profile of v1, /device:TPU:32, one launch (start us, length us, event | category | flops | bytes accessed | tf_op | source)
XLA Modules:
  0.0 399.9 jit_solution(10126933862395973096)
XLA Ops:
  8.2 1.9 collective-permute-start
  12.7 16.1 %all-to-all-start = ((bf16[1,128,1,4,256]{4,3,2,0,1:T(4,128)(2,1)}), bf16[1,128,1,4,256]{4,3,2,0,1:T(4,128)(2,1)S(1)}, u32[]{:S(2)}, u32[]{:S(2)}) async-start(bf16[1,128,1,4,256]{4,3,2,0,1:T(4,128)(2,1)} %bitcast.1), calls=%async_computation | async-start | bytes 524288 | tf_op jit(solution)/shard_map/all_to_all | solution.py:62
  30.7 6.0 %copy.49 = bf16[3,3,3,256,256]{3,4,2,1,0:T(8,128)(2,1)} copy(bf16[3,3,3,256,256]{4,3,2,1,0:T(8,128)(2,1)} %param.9) | data formatting | bytes 7077888 | tf_op args[1]
  36.7 4.3 %rev.3 = bf16[3,3,3,256,256]{3,4,2,1,0:T(8,128)(2,1)} reverse(bf16[3,3,3,256,256]{3,4,2,1,0:T(8,128)(2,1)} %copy.49), dimensions={0,1,2} | reverse | bytes 7077888 | tf_op jit(solution)/shard_map/rev | solution.py:70
  41.0 4.2 %reverse_bitcast_fusion = bf16[3,3,3,256,256]{4,3,2,1,0:T(8,128)(2,1)} fusion(bf16[3,3,3,256,256]{3,4,2,1,0:T(8,128)(2,1)} %copy.49), kind=kLoop, calls=%fused_computation.239 | loop fusion | bytes 7077888 | tf_op jit(solution)/shard_map/transpose | solution.py:70
  45.5 4.1 %pad_slice_fusion.24 = (bf16[4,32,4,256]{3,2,1,0:T(4,128)(2,1)}, bf16[4,32,4,256]{3,2,1,0:T(4,128)(2,1)}, bf16[4,32,4,256]{3,2,1,0:T(4,128)(2,1)}, bf16[4,32,4,2...) fusion(bf16[6,32,4,256]{3,2,1,0:T(4,128)(2,1)S(1)} %pad_maximum, ...), kind=kLoop, calls=%fused_computation.52 | loop fusion | bytes 5373952 | tf_op jit(solution)/shard_map/slice | solution.py:22
  51.5 1.7 concatenate.77
  54.0 1.8 concatenate.78
  55.8 1.7 concatenate.79
  58.3 1.7 concatenate.81
  66.9 1.7 concatenate.86
  70.3 1.7 concatenate.88
  72.8 1.7 concatenate.90
  76.2 1.7 concatenate.92
  86.1 1.8 constant_dynamic-update-slice_fusion.26
  87.9 1.7 constant_dynamic-update-slice_fusion.25
  119.5 6.1 %multiply_convert_fusion = (bf16[512,256]{1,0:T(8,128)(2,1)S(1)}, bf16[512,256]{1,0:T(8,128)(2,1)S(1)}) fusion(f32[512,256]{1,0:T(8,128)S(1)} %reshape.133, bf16[512,6912]{1,0:T(8,128)(2,1)} %constant_dynamic-update-slice_fusion.1, bf16[6912,256]{1,0:T(8,128)(2,1)} %bitcast.233), kind=kOutput, calls=%fused_computation.102 | convolution fusion | flops 1813381120 | bytes 11665408 | tf_op jit(solution)/shard_map/dot_general | solution.py:31
  145.1 12.2 %all-to-all-start.1 = ((bf16[32,1,4,1,4,256]{5,4,2,3,1,0:T(4,128)(2,1)}), bf16[32,1,4,1,4,256]{5,4,2,3,1,0:T(4,128)(2,1)S(1)}, u32[]{:S(2)}, u32[]{:S(2)}) async-start(bf16[32,1,4,1,4,256]{5,4,2,3,1,0:T(4,128)(2,1)} %constant_dynamic-update-slice_fusion.29), calls=%async_computation.1 | async-start | bytes 524288 | tf_op jit(solution)/shard_map/all_to_all | solution.py:53
  157.4 2.0 collective-permute-start.1
  159.6 10.0 %collective-permute-done.1 = bf16[2,32,4,256]{3,1,2,0:T(8,128)(2,1)S(1)} collective-permute-done((bf16[2,32,4,256]{3,1,2,0:T(8,128)(2,1)S(1)}, bf16[2,32,4,256]{3,1,2,0:T(8,128)(2,1)S(1)}, u32[]{:S(2)}, u32[]{:S(2)}) %collective-permute-start.1) | collective-permute-done | bytes 131104 | tf_op jit(solution)/shard_map/ppermute | solution.py:11
  192.4 6.0 %fusion.52 = f32[4,32,4,256]{3,1,2,0:T(8,128)S(1)} fusion(bf16[4,32,4,6912]{3,1,2,0:T(8,128)(2,1)} %fusion.49, bf16[6912,256,1,1]{1,0,3,2:T(8,128)(2,1)} %bitcast.234), kind=kOutput, calls=%fused_computation.241 | convolution fusion | flops 1811939328 | bytes 11141120 | tf_op jit(solution)/shard_map/dot_general | solution.py:31
  198.5 104.5 %reduce-scatter.5.cloned.1.call-done = f32[8,1024]{1,0:T(8,128)} async-done(((f32[256,1024]{1,0:T(8,128)}), f32[8,1024]{1,0:T(8,128)}) %reduce-scatter.5.cloned.1.call-update) | async-done | bytes 32784 | tf_op jit(solution)/shard_map/reduce_scatter | solution.py:89
  302.9 1.8 copy.84
  305.7 85.9 %reduce-scatter.7.cloned.1.call-done = f32[64,8]{1,0:T(8,128)} async-done(((f32[1024,8]{1,0:T(8,128)}), f32[64,8]{1,0:T(8,128)}) %reduce-scatter.7.cloned.1.call-update) | async-done | bytes 2064
  (159 shorter events, 103.0 us)
Async XLA Ops:
  7.2 4.3 %copy-start = (bf16[256,1024]{1,0:T(8,128)(2,1)S(1)}, bf16[256,1024]{1,0:T(8,128)(2,1)}, u32[]{:S(2)}) copy-start(bf16[256,1024]{1,0:T(8,128)(2,1)} %param.10) | copy-start | bytes 1572868
  8.2 37.1 %collective-permute-start = (bf16[2,32,4,256]{3,2,1,0:T(4,128)(2,1)S(1)}, bf16[2,32,4,256]{3,2,1,0:T(4,128)(2,1)S(1)}, u32[]{:S(2)}, u32[]{:S(2)}) collective-permute-start(bf16[2,32,4,256]{3,2,1,0:T(4,128)(2,1)S(1)} %slice_bitcast_fusion), channel_id=1, source_target_pairs={{0,16},{16,32},{32,48},{48,64},{64,80},{80,96},{96,112},{112,128},... | collective-permute-start | bytes 393224 | tf_op jit(solution)/shard_map/ppermute | solution.py:11
  12.7 106.5 %all-to-all-start = ((bf16[1,128,1,4,256]{4,3,2,0,1:T(4,128)(2,1)}), bf16[1,128,1,4,256]{4,3,2,0,1:T(4,128)(2,1)S(1)}, u32[]{:S(2)}, u32[]{:S(2)}) async-start(bf16[1,128,1,4,256]{4,3,2,0,1:T(4,128)(2,1)} %bitcast.1), calls=%async_computation | async-start | bytes 524288 | tf_op jit(solution)/shard_map/all_to_all | solution.py:62
  36.7 8.6 %copy-start.1 = (bf16[1,4,32,4,256]{4,3,2,1,0:T(4,128)(2,1)S(1)}, bf16[1,4,32,4,256]{4,3,2,1,0:T(4,128)(2,1)}, u32[]{:S(2)}) copy-start(bf16[1,4,32,4,256]{4,3,2,1,0:T(4,128)(2,1)} %param.8) | copy-start | bytes 786436
  53.3 29.8 %copy-start.10 = (bf16[4,32,4,256]{3,2,1,0:T(4,128)(2,1)S(1)}, bf16[4,32,4,256]{3,2,1,0:T(4,128)(2,1)}, u32[]{:S(2)}) copy-start(bf16[4,32,4,256]{3,2,1,0:T(4,128)(2,1)} %get-tuple-element.49) | copy-start | bytes 786436
  54.0 29.9 %copy-start.8 = (bf16[4,32,4,256]{3,2,1,0:T(4,128)(2,1)S(1)}, bf16[4,32,4,256]{3,2,1,0:T(4,128)(2,1)}, u32[]{:S(2)}) copy-start(bf16[4,32,4,256]{3,2,1,0:T(4,128)(2,1)} %get-tuple-element.53) | copy-start | bytes 786436
  58.3 25.6 %copy-start.9 = (bf16[4,32,4,256]{3,2,1,0:T(4,128)(2,1)S(1)}, bf16[4,32,4,256]{3,2,1,0:T(4,128)(2,1)}, u32[]{:S(2)}) copy-start(bf16[4,32,4,256]{3,2,1,0:T(4,128)(2,1)} %get-tuple-element.52) | copy-start | bytes 786436
  86.1 23.9 %copy-start.7 = (bf16[512,256]{1,0:T(8,128)(2,1)S(1)}, bf16[512,256]{1,0:T(8,128)(2,1)}, u32[]{:S(2)}) copy-start(bf16[512,256]{1,0:T(8,128)(2,1)} %concatenate.91) | copy-start | bytes 786436
  86.1 24.7 %copy-start.6 = (bf16[512,256]{1,0:T(8,128)(2,1)S(1)}, bf16[512,256]{1,0:T(8,128)(2,1)}, u32[]{:S(2)}) copy-start(bf16[512,256]{1,0:T(8,128)(2,1)} %concatenate.92) | copy-start | bytes 786436
  86.1 25.4 %copy-start.5 = (bf16[512,256]{1,0:T(8,128)(2,1)S(1)}, bf16[512,256]{1,0:T(8,128)(2,1)}, u32[]{:S(2)}) copy-start(bf16[512,256]{1,0:T(8,128)(2,1)} %concatenate.93) | copy-start | bytes 786436
  86.1 26.2 %copy-start.4 = (bf16[512,256]{1,0:T(8,128)(2,1)S(1)}, bf16[512,256]{1,0:T(8,128)(2,1)}, u32[]{:S(2)}) copy-start(bf16[512,256]{1,0:T(8,128)(2,1)} %concatenate.94) | copy-start | bytes 786436
  86.1 26.9 %copy-start.3 = (bf16[512,256]{1,0:T(8,128)(2,1)S(1)}, bf16[512,256]{1,0:T(8,128)(2,1)}, u32[]{:S(2)}) copy-start(bf16[512,256]{1,0:T(8,128)(2,1)} %concatenate.95) | copy-start | bytes 786436
  86.1 27.7 %copy-start.2 = (bf16[512,256]{1,0:T(8,128)(2,1)S(1)}, bf16[512,256]{1,0:T(8,128)(2,1)}, u32[]{:S(2)}) copy-start(bf16[512,256]{1,0:T(8,128)(2,1)} %concatenate.96) | copy-start | bytes 786436
  145.1 39.4 %all-to-all-start.1 = ((bf16[32,1,4,1,4,256]{5,4,2,3,1,0:T(4,128)(2,1)}), bf16[32,1,4,1,4,256]{5,4,2,3,1,0:T(4,128)(2,1)S(1)}, u32[]{:S(2)}, u32[]{:S(2)}) async-start(bf16[32,1,4,1,4,256]{5,4,2,3,1,0:T(4,128)(2,1)} %constant_dynamic-update-slice_fusion.29), calls=%async_computation.1 | async-start | bytes 524288 | tf_op jit(solution)/shard_map/all_to_all | solution.py:53
  157.2 145.7 %reduce-scatter.5.cloned.1.call-start = ((), (), s32[]{:S(2)}) async-start(), calls=%async_computation.4 | async-start | bytes 1081344 | tf_op jit(solution)/shard_map/reduce_scatter | solution.py:89
  157.4 12.2 %collective-permute-start.1 = (bf16[2,32,4,256]{3,1,2,0:T(8,128)(2,1)S(1)}, bf16[2,32,4,256]{3,1,2,0:T(8,128)(2,1)S(1)}, u32[]{:S(2)}, u32[]{:S(2)}) collective-permute-start(bf16[2,32,4,256]{3,1,2,0:T(8,128)(2,1)S(1)} %copy.46), channel_id=1, source_target_pairs={{16,0},{32,16},{48,32},{64,48},{80,64},{96,80},{112,96},{128,112},... | collective-permute-start | bytes 393224 | tf_op jit(solution)/shard_map/ppermute | solution.py:11
  186.0 205.6 %reduce-scatter.7.cloned.1.call-start = ((), (), s32[]{:S(2)}) async-start(), calls=%async_computation.5 | async-start | bytes 557056
Sparse Core Ops, SparseCore 0:
  186.1 116.7 reduce-scatter.4
  305.9 85.6 reduce-scatter.6
